TPU v7x, 32 devices: a whole 2x2x4 slice. The times are simulated.
32 devices in a mesh: dp: 16 (over z, y, core), tm: 2 (over x).
Axes of the slice: x: 2, y: 2, z: 4, core: 2. Of those that a mesh axis runs over, the one named last changes fastest.
Arguments:
- hidden_in: bfloat16 [2, 16, 512, 1024], P(None, 'dp', 'tm'), may hold values from -6 to 6
- memory: bfloat16 [2, 16, 512, 1024], P(None, 'dp', 'tm'), may hold values from -6 to 6
- compressed_in: bfloat16 [2, 16, 512, 1024], P(None, 'dp', 'tm'), may hold values from -6 to 6
- lengths: int32 [2, 16], P(None, 'dp'), may hold values from 128 to 512, as said below
- gain_attn: bfloat16 [1024], P(('dp', 'tm')), may hold values from 0.099609375 to 1.8984375
- gain_ffn: bfloat16 [1024], P(('dp', 'tm')), may hold values from 0.099609375 to 1.8984375
- w_query: bfloat16 [1024, 1024], P(None, ('dp', 'tm')), may hold values from -0.1875 to 0.1875
- w_key: bfloat16 [1024, 1024], P(None, ('dp', 'tm')), may hold values from -0.1875 to 0.1875
- w_value: bfloat16 [1024, 1024], P(None, ('dp', 'tm')), may hold values from -0.1875 to 0.1875
- w_out: bfloat16 [1024, 1024], P(None, ('dp', 'tm')), may hold values from -4 to 4
- w_up: bfloat16 [1024, 4096], P(None, ('dp', 'tm')), may hold values from -0.1875 to 0.1875
- w_down: bfloat16 [4096, 1024], P(None, ('dp', 'tm')), may hold values from -0.125 to 0.125
- w_compress: bfloat16 [2048, 1024], P(None, ('dp', 'tm')), may hold values from -0.125 to 0.125
- cot_out: bfloat16 [2, 16, 512, 1024], P(None, 'dp', 'tm'), may hold values from -6 to 6
- cot_comp: bfloat16 [2, 16, 256, 1024], P(None, 'dp', 'tm'), may hold values from -6 to 6
Outputs:
- layer_out: bfloat16 [2, 16, 512, 1024], P(None, 'dp', 'tm')
- compressed: bfloat16 [2, 16, 256, 1024], P(None, 'dp', 'tm')
- grad_in: bfloat16 [2, 16, 512, 1024], P(None, 'dp', 'tm')
- grad_gain_attn: float32 [1024], P(('dp', 'tm'))
- grad_gain_ffn: float32 [1024], P(('dp', 'tm'))
- grad_query: float32 [1024, 1024], P(None, ('dp', 'tm'))
- grad_key: float32 [1024, 1024], P(None, ('dp', 'tm'))
- grad_value: float32 [1024, 1024], P(None, ('dp', 'tm'))
- grad_out: float32 [1024, 1024], P(None, ('dp', 'tm'))
- grad_up: float32 [1024, 4096], P(None, ('dp', 'tm'))
- grad_down: float32 [4096, 1024], P(None, ('dp', 'tm'))
- grad_compress: float32 [2048, 1024], P(None, ('dp', 'tm'))
Inputs may be any that keep to these rules, and one draw needn't show every extreme that they name: `lengths`: each length is a quarter of 512, half of 512 or 512. In each micro-batch at least one stream has length 512.
All inputs are finite; a program needn't handle non-finite values.
Results may differ from a plain program's by a relative error of at most 0.014.
Values may be sent and summed in bfloat16 or wider, within the bound.
No kernel may reach another device: no remote copies, remote signals or barrier semaphores. Data moves between devices by JAX's collectives and lax.ppermute only.
A program may use at most 256 MiB of HBM per device.

v0:
```python
import math

import jax
import jax.numpy as jnp
from jax import lax
from jax.sharding import PartitionSpec as P

H = 8
DH = 128
MEM = 512
CMEM = 512
COMP = 2


EPSILON = 1e-05
ROPE_BASE = 10000.0
NEG_LARGE = -1e30


def passed_along(value, axis, steps):
    count = lax.axis_size(axis)
    leading, last = (max(0, -steps), min(count, count - steps))
    return lax.ppermute(value, axis, [(source, source + steps) for source in range(leading, last)])


def layer_norm(values, gain):
    centre = values - jnp.mean(values, axis=-1, keepdims=True)
    spread = jnp.mean(centre * centre, axis=-1, keepdims=True)
    return centre * lax.rsqrt(spread + EPSILON) * gain


def rotate(values, positions):
    half_size = DH // 2
    frequency = jnp.exp(
        jnp.arange(half_size, dtype=jnp.float32) * (-2.0 * math.log(ROPE_BASE) / DH)
    )
    angles = positions.astype(jnp.float32)[:, None] * frequency[None, :]
    cosine = jnp.cos(angles)[:, None, :]
    sine_part = jnp.sin(angles)[:, None, :]
    per_head = values.reshape(values.shape[:-1] + (H, DH))
    front_half = per_head[..., :half_size]
    back_half = per_head[..., half_size:]
    turned = jnp.concatenate(
        [front_half * cosine - back_half * sine_part, back_half * cosine + front_half * sine_part],
        axis=-1,
    )
    return turned.reshape(values.shape)


def gelu_tanh(values):
    inner = math.sqrt(2.0 / math.pi) * (values + 0.044715 * values * values * values)
    return 0.5 * values * (1.0 + jnp.tanh(inner))


def project(row_block, weight):
    return jnp.einsum("brd,de->bre", row_block, weight, preferred_element_type=jnp.float32)


def weight_grad(left, right):
    return jnp.einsum("brd,bre->de", left, right, preferred_element_type=jnp.float32)


def back_project(grads, weight):
    return jnp.einsum("bre,de->brd", grads, weight, preferred_element_type=jnp.float32)


def exact_grad(left, right):
    return jnp.einsum(
        "brd,bre->de",
        left,
        right,
        precision=lax.Precision.HIGHEST,
        preferred_element_type=jnp.float32,
    )


def exact_back(grads, weight):
    return jnp.einsum(
        "bre,de->brd",
        grads,
        weight,
        precision=lax.Precision.HIGHEST,
        preferred_element_type=jnp.float32,
    )


def local(
    hidden_in,
    memory,
    compressed_in,
    lengths,
    gain_attn,
    gain_ffn,
    w_query,
    w_key,
    w_value,
    w_out,
    w_up,
    w_down,
    w_compress,
    cot_out,
    cot_comp,
):
    micro_count, stream_count, block_len, width = hidden_in.shape
    mem_block = memory.shape[2]
    cmem_block = compressed_in.shape[2]
    time_index = lax.axis_index("tm")
    time_size = lax.axis_size("tm")
    cmem_total = cmem_block * time_size
    mem_total = mem_block * time_size
    front_keys = (cmem_block + mem_block) * time_size
    seq_total = block_len * time_size
    key_count = front_keys + seq_total
    score_scale = 1.0 / math.sqrt(DH)
    rim_rows = COMP - 1
    window_count = block_len // COMP
    shards = (
        gain_attn.reshape(1, -1),
        gain_ffn.reshape(1, -1),
        w_query,
        w_key,
        w_value,
        w_out,
        w_up,
        w_down,
        w_compress,
    )
    query_pos = time_index * block_len + jnp.arange(block_len, dtype=jnp.int32)
    key_pos_all = jnp.concatenate(
        [
            COMP * (jnp.arange(cmem_total, dtype=jnp.int32) - CMEM) - MEM,
            jnp.arange(mem_total, dtype=jnp.int32) - MEM,
            jnp.arange(seq_total, dtype=jnp.int32),
        ]
    )
    window_end = time_index * block_len + COMP * jnp.arange(window_count, dtype=jnp.int32)
    key_rank = jnp.arange(key_count, dtype=jnp.int32) - front_keys
    allowed = (key_rank[None, :] <= query_pos[:, None])[None, None]
    layer_outs = []
    comp_outs = []
    grad_outs = []
    shard_sums = None
    for micro_step in range(micro_count):
        gathered = (
            lax.all_gather(shards[0], ("dp", "tm"), axis=1, tiled=True),
            lax.all_gather(shards[1], ("dp", "tm"), axis=1, tiled=True),
            lax.all_gather(shards[2], ("dp", "tm"), axis=1, tiled=True),
            lax.all_gather(shards[3], ("dp", "tm"), axis=1, tiled=True),
            lax.all_gather(shards[4], ("dp", "tm"), axis=1, tiled=True),
            lax.all_gather(shards[5], ("dp", "tm"), axis=1, tiled=True),
            lax.all_gather(shards[6], ("dp", "tm"), axis=1, tiled=True),
            lax.all_gather(shards[7], ("dp", "tm"), axis=1, tiled=True),
            lax.all_gather(shards[8], ("dp", "tm"), axis=1, tiled=True),
        )
        (
            gain_row_attn,
            gain_row_ffn,
            query_full,
            key_full,
            value_full,
            out_full,
            up_full,
            down_full,
            compress_full,
        ) = gathered
        gain_first = gain_row_attn.reshape(-1).astype(jnp.float32)
        gain_second = gain_row_ffn.reshape(-1).astype(jnp.float32)
        stream_lens = lengths[micro_step]
        row_mask = (query_pos[None, :] < stream_lens[:, None]).astype(jnp.float32)[..., None]
        window_mask = (window_end[None, :] < stream_lens[:, None]).astype(jnp.float32)[..., None]
        inputs = hidden_in[micro_step].astype(jnp.float32)
        normed, norm_pull = jax.vjp(layer_norm, inputs, gain_first)
        normed_low = normed.astype(jnp.bfloat16)
        left_rim = passed_along(normed_low[:, block_len - rim_rows :], "tm", 1)
        padded = jnp.concatenate([left_rim, normed_low], axis=1)
        windows = padded[:, :block_len].reshape(stream_count, window_count, COMP * width)
        compressed = project(windows, compress_full) * window_mask
        comp_outs.append(compressed.astype(jnp.bfloat16))
        mem_rows = memory[micro_step]
        cmem_rows = compressed_in[micro_step]
        queries = rotate(project(normed_low, query_full), query_pos).astype(jnp.bfloat16)
        source_parts = (
            lax.all_gather(cmem_rows, "tm", axis=1, tiled=True),
            lax.all_gather(mem_rows, "tm", axis=1, tiled=True),
            lax.all_gather(normed_low, "tm", axis=1, tiled=True),
        )
        source_all = jnp.concatenate(source_parts, axis=1)
        key_all = (
            rotate(project(source_all, key_full), key_pos_all)
            .astype(jnp.bfloat16)
            .reshape(stream_count, key_count, H, DH)
        )
        value_all = (
            project(source_all, value_full)
            .astype(jnp.bfloat16)
            .reshape(stream_count, key_count, H, DH)
        )
        query_heads = queries.reshape(stream_count, block_len, H, DH)
        scores = (
            jnp.einsum("bthd,bjhd->bhtj", query_heads, key_all, preferred_element_type=jnp.float32)
            * score_scale
        )
        masked = jnp.where(allowed, scores, NEG_LARGE)
        top_score = jnp.max(masked, axis=-1, keepdims=True)
        exp_scores = jnp.exp(masked - top_score)
        row_total = jnp.sum(exp_scores, axis=-1, keepdims=True)
        log_total = top_score + jnp.log(row_total)
        attn_low = (exp_scores / row_total).astype(jnp.bfloat16)
        context = jnp.einsum(
            "bhtj,bjhd->bthd", attn_low, value_all, preferred_element_type=jnp.float32
        )
        context = context.reshape(stream_count, block_len, width).astype(jnp.bfloat16)
        middle = inputs + project(context, out_full)
        normed_ffn, ffn_pull = jax.vjp(layer_norm, middle, gain_second)
        ffn_low = normed_ffn.astype(jnp.bfloat16)
        upper = project(ffn_low, up_full)
        active, gelu_pull = jax.vjp(gelu_tanh, upper)
        active_low = active.astype(jnp.bfloat16)
        branch = project(active_low, down_full)
        layer_outs.append(((middle + branch) * row_mask).astype(jnp.bfloat16))
        grad_live = cot_out[micro_step].astype(jnp.float32) * row_mask
        grad_branch = grad_live.astype(jnp.bfloat16)
        grad_down = weight_grad(active_low, grad_branch)
        grad_active = back_project(grad_branch, down_full)
        grad_upper = gelu_pull(grad_active)[0].astype(jnp.bfloat16)
        grad_up = weight_grad(ffn_low, grad_upper)
        grad_ffn_norm = back_project(grad_upper, up_full)
        grad_middle_norm, grad_gain_ffn = ffn_pull(grad_ffn_norm)
        grad_middle = grad_live + grad_middle_norm
        grad_attended = grad_middle.astype(jnp.bfloat16)
        grad_outproj = weight_grad(context, grad_attended)
        grad_context = back_project(grad_attended, out_full).astype(jnp.bfloat16)
        context_heads = grad_context.reshape(stream_count, block_len, H, DH)
        scores_again = (
            jnp.einsum("bthd,bjhd->bhtj", query_heads, key_all, preferred_element_type=jnp.float32)
            * score_scale
        )
        attn_again = jnp.exp(jnp.where(allowed, scores_again, NEG_LARGE) - log_total)
        grad_attn = jnp.einsum(
            "bthd,bjhd->bhtj", context_heads, value_all, preferred_element_type=jnp.float32
        )
        inner_sum = jnp.sum(attn_again * grad_attn, axis=-1, keepdims=True)
        grad_scores = (attn_again * (grad_attn - inner_sum)).astype(jnp.bfloat16)
        grad_queries = (
            jnp.einsum("bhtj,bjhd->bthd", grad_scores, key_all, preferred_element_type=jnp.float32)
            * score_scale
        )
        grad_keys = (
            jnp.einsum(
                "bhtj,bthd->bjhd", grad_scores, query_heads, preferred_element_type=jnp.float32
            )
            * score_scale
        )
        grad_keys = grad_keys.reshape(stream_count, key_count, width)
        grad_vals = jnp.einsum(
            "bhtj,bthd->bjhd",
            attn_again.astype(jnp.bfloat16),
            context_heads,
            preferred_element_type=jnp.float32,
        )
        grad_vals = grad_vals.reshape(stream_count, key_count, width)
        grad_query_lin = rotate(
            grad_queries.reshape(stream_count, block_len, width), -query_pos
        ).astype(jnp.bfloat16)
        grad_query = weight_grad(normed_low, grad_query_lin)
        grad_normed = back_project(grad_query_lin, query_full)
        key_turned = rotate(grad_keys, -key_pos_all)
        grad_key = exact_grad(source_all, key_turned)
        grad_value = exact_grad(source_all, grad_vals)
        token_terms = exact_back(key_turned[:, front_keys:], key_full) + exact_back(
            grad_vals[:, front_keys:], value_full
        )
        grad_normed = grad_normed + lax.psum_scatter(
            token_terms.astype(jnp.bfloat16), "tm", scatter_dimension=1, tiled=True
        ).astype(jnp.float32)
        comp_grad = (cot_comp[micro_step].astype(jnp.float32) * window_mask).astype(jnp.bfloat16)
        grad_compress = weight_grad(windows, comp_grad)
        grad_windows = back_project(comp_grad, compress_full).reshape(
            stream_count, block_len, width
        )
        rim_grad = passed_along(grad_windows[:, :rim_rows], "tm", -1)
        grad_normed = grad_normed + jnp.concatenate([grad_windows[:, rim_rows:], rim_grad], axis=1)
        grad_inputs_norm, grad_gain_attn = norm_pull(grad_normed)
        grad_outs.append((grad_middle + grad_inputs_norm).astype(jnp.bfloat16))
        micro_grads = (
            grad_gain_attn.reshape(1, -1),
            grad_gain_ffn.reshape(1, -1),
            grad_query,
            grad_key,
            grad_value,
            grad_outproj,
            grad_up,
            grad_down,
            grad_compress,
        )
        micro_shares = (
            lax.psum_scatter(micro_grads[0], ("dp", "tm"), scatter_dimension=1, tiled=True),
            lax.psum_scatter(micro_grads[1], ("dp", "tm"), scatter_dimension=1, tiled=True),
            lax.psum_scatter(micro_grads[2], ("dp", "tm"), scatter_dimension=1, tiled=True),
            lax.psum_scatter(micro_grads[3], ("dp", "tm"), scatter_dimension=1, tiled=True),
            lax.psum_scatter(micro_grads[4], ("dp", "tm"), scatter_dimension=1, tiled=True),
            lax.psum_scatter(micro_grads[5], ("dp", "tm"), scatter_dimension=1, tiled=True),
            lax.psum_scatter(micro_grads[6], ("dp", "tm"), scatter_dimension=1, tiled=True),
            lax.psum_scatter(micro_grads[7], ("dp", "tm"), scatter_dimension=1, tiled=True),
            lax.psum_scatter(micro_grads[8], ("dp", "tm"), scatter_dimension=1, tiled=True),
        )
        shard_sums = (
            micro_shares if shard_sums is None else jax.tree.map(jnp.add, shard_sums, micro_shares)
        )
    return (
        jnp.stack(layer_outs),
        jnp.stack(comp_outs),
        jnp.stack(grad_outs),
        shard_sums[0].reshape(-1),
        shard_sums[1].reshape(-1),
        shard_sums[2],
        shard_sums[3],
        shard_sums[4],
        shard_sums[5],
        shard_sums[6],
        shard_sums[7],
        shard_sums[8],
    )


def solution(mesh):
    return jax.shard_map(
        local,
        mesh=mesh,
        in_specs=(
            P(None, "dp", "tm", None),
            P(None, "dp", "tm", None),
            P(None, "dp", "tm", None),
            P(None, "dp"),
            P(("dp", "tm")),
            P(("dp", "tm")),
            P(None, ("dp", "tm")),
            P(None, ("dp", "tm")),
            P(None, ("dp", "tm")),
            P(None, ("dp", "tm")),
            P(None, ("dp", "tm")),
            P(None, ("dp", "tm")),
            P(None, ("dp", "tm")),
            P(None, "dp", "tm", None),
            P(None, "dp", "tm", None),
        ),
        out_specs=(
            P(None, "dp", "tm", None),
            P(None, "dp", "tm", None),
            P(None, "dp", "tm", None),
            P(("dp", "tm")),
            P(("dp", "tm")),
            P(None, ("dp", "tm")),
            P(None, ("dp", "tm")),
            P(None, ("dp", "tm")),
            P(None, ("dp", "tm")),
            P(None, ("dp", "tm")),
            P(None, ("dp", "tm")),
            P(None, ("dp", "tm")),
        ),
        check_vma=False,
    )
```

profile of v0, /device:TPU:0, one launch (start us, length us, event | category | flops | bytes accessed | tf_op | source)
XLA Modules:
  0.0 2455.7 jit_solution(8872828626143868919)
XLA Ops:
  9.7 42.0 %all-reduce.2 = (bf16[1024]{0:T(1024)(128)(2,1)S(1)}, bf16[1024]{0:T(1024)(128)(2,1)S(1)}) all-reduce(bf16[1024]{0:T(1024)(128)(2,1)S(1)} %dynamic-update-slice, bf16[1024]{0:T(1024)(128)(2,1)S(1)} %dynamic-update-slice.1), channel_id=4, replica_groups=mesh['dp'=16,'tm'=2] {'dp','tm'}, use_global_device_ids=true, to_apply=%add | all-reduce | flops 2048 | bytes 8192
  92.6 23.5 all-gather.44.cloned.1.call-done
  116.0 22.7 all-gather.42.cloned.1.call-done
  138.8 59.4 %all-gather.26.cloned.1.call-done = bf16[1024,1024]{0,1:T(8,128)(2,1)} async-done(((bf16[1024,32]{0,1:T(8,128)(2,1)}), bf16[1024,1024]{0,1:T(8,128)(2,1)}) %all-gather.26.cloned.1.call-update) | async-done | bytes 2097168 | tf_op jit(solution)/shard_map/all_gather | solution.py:148
  206.7 13.6 all-gather.20.cloned.1.call-done
  220.3 23.5 all-gather.40.cloned.1.call-done
  243.8 23.5 all-gather.38.cloned.1.call-done
  284.0 42.7 %all-gather.22.cloned.1.call-done = bf16[1024,1024]{0,1:T(8,128)(2,1)} async-done(((bf16[1024,32]{0,1:T(8,128)(2,1)}), bf16[1024,1024]{0,1:T(8,128)(2,1)}) %all-gather.22.cloned.1.call-update) | async-done | bytes 2097168 | tf_op jit(solution)/shard_map/all_gather | solution.py:149
  338.7 46.3 %all-gather.28.cloned.1.call-done = bf16[1024,1024]{0,1:T(8,128)(2,1)} async-done(((bf16[1024,32]{0,1:T(8,128)(2,1)}), bf16[1024,1024]{0,1:T(8,128)(2,1)}) %all-gather.28.cloned.1.call-update) | async-done | bytes 2097168 | tf_op jit(solution)/shard_map/all_gather | solution.py:150
  406.8 72.2 %all-gather.30.cloned.1.call-done = bf16[1024,4096]{1,0:T(8,128)(2,1)} async-done(((bf16[1024,128]{1,0:T(8,128)(2,1)}), bf16[1024,4096]{1,0:T(8,128)(2,1)}) %all-gather.30.cloned.1.call-update) | async-done | bytes 8388624 | tf_op jit(solution)/shard_map/all_gather | solution.py:151
  491.7 65.7 %all-gather.32.cloned.1.call-done = bf16[4096,1024]{0,1:T(8,128)(2,1)} async-done(((bf16[4096,32]{0,1:T(8,128)(2,1)}), bf16[4096,1024]{0,1:T(8,128)(2,1)}) %all-gather.32.cloned.1.call-update) | async-done | bytes 8388624 | tf_op jit(solution)/shard_map/all_gather | solution.py:152
  738.2 12.8 fusion.31
  751.0 13.6 fusion.46
  770.6 12.8 fusion.29
  783.5 13.5 fusion.49
  798.2 10.7 fusion.148
  859.8 117.4 %reduce-scatter.34.cloned.1.call-done = f32[32,1]{1,0:T(8,128)} async-done(((f32[1024,1]{1,0:T(8,128)}), f32[32,1]{1,0:T(8,128)}) %reduce-scatter.34.cloned.1.call-update) | async-done | bytes 144
  978.5 180.5 %reduce-scatter.32.cloned.1.call-done = f32[2048,32]{0,1:T(8,128)} async-done(((f32[2048,1024]{0,1:T(8,128)}), f32[2048,32]{0,1:T(8,128)}) %reduce-scatter.32.cloned.1.call-update) | async-done | bytes 262160 | tf_op jit(solution)/shard_map/reduce_scatter | solution.py:305
  1159.0 146.1 %reduce-scatter.26.cloned.1.call-done = f32[1024,32]{0,1:T(8,128)} async-done(((f32[1024,1024]{0,1:T(8,128)}), f32[1024,32]{0,1:T(8,128)}) %reduce-scatter.26.cloned.1.call-update) | async-done | bytes 131088 | tf_op jit(solution)/shard_map/reduce_scatter | solution.py:302
  1305.1 142.1 %reduce-scatter.24.cloned.1.call-done = f32[1024,32]{0,1:T(8,128)} async-done(((f32[1024,1024]{0,1:T(8,128)}), f32[1024,32]{0,1:T(8,128)}) %reduce-scatter.24.cloned.1.call-update) | async-done | bytes 131088 | tf_op jit(solution)/shard_map/reduce_scatter | solution.py:301
  1447.2 141.3 %reduce-scatter.20.cloned.1.call-done = f32[1024,32]{0,1:T(8,128)} async-done(((f32[1024,1024]{0,1:T(8,128)}), f32[1024,32]{0,1:T(8,128)}) %reduce-scatter.20.cloned.1.call-update) | async-done | bytes 131088 | tf_op jit(solution)/shard_map/reduce_scatter | solution.py:299
  1588.5 141.9 %reduce-scatter.22.cloned.1.call-done = f32[1024,32]{0,1:T(8,128)} async-done(((f32[1024,1024]{0,1:T(8,128)}), f32[1024,32]{0,1:T(8,128)}) %reduce-scatter.22.cloned.1.call-update) | async-done | bytes 131088 | tf_op jit(solution)/shard_map/reduce_scatter | solution.py:300
  1730.4 356.8 %reduce-scatter.30.cloned.1.call-done = f32[4096,32]{0,1:T(8,128)} async-done(((f32[4096,1024]{0,1:T(8,128)}), f32[4096,32]{0,1:T(8,128)}) %reduce-scatter.30.cloned.1.call-update) | async-done | bytes 524304 | tf_op jit(solution)/shard_map/reduce_scatter | solution.py:304
  2087.2 361.4 %reduce-scatter.28.cloned.1.call-done = f32[1024,128]{1,0:T(8,128)} async-done(((f32[1024,4096]{1,0:T(8,128)}), f32[1024,128]{1,0:T(8,128)}) %reduce-scatter.28.cloned.1.call-update) | async-done | bytes 524304 | tf_op jit(solution)/shard_map/reduce_scatter | solution.py:303
  (478 shorter events, 353.3 us)
Async XLA Ops:
  7.2 78.3 %all-gather.24.cloned.1.call-start = ((), (), s32[]{:S(2)}) async-start(), calls=%async_computation.13 | async-start | bytes 2162688 | tf_op jit(solution)/shard_map/all_gather | solution.py:147
  7.9 84.6 %all-gather.34.cloned.1.call-start = ((), (), s32[]{:S(2)}) async-start(), calls=%async_computation.18 | async-start | bytes 1572864 | tf_op jit(solution)/shard_map/all_gather | solution.py:185
  59.1 79.7 %all-gather.42.cloned.1.call-start = ((), (), s32[]{:S(2)}) async-start(), calls=%async_computation.24 | async-start | bytes 1572864 | tf_op jit(solution)/shard_map/all_gather | solution.py:183
  60.2 137.9 %all-gather.26.cloned.1.call-start = ((), (), s32[]{:S(2)}) async-start(), calls=%async_computation.14 | async-start | bytes 2162688 | tf_op jit(solution)/shard_map/all_gather | solution.py:148
  60.8 159.5 %all-gather.20.cloned.1.call-start = ((), (), s32[]{:S(2)}) async-start(), calls=%async_computation.11 | async-start | bytes 1572864 | tf_op jit(solution)/shard_map/all_gather | solution.py:185
  61.4 182.4 %all-gather.40.cloned.1.call-start = ((), (), s32[]{:S(2)}) async-start(), calls=%async_computation.23 | async-start | bytes 1572864 | tf_op jit(solution)/shard_map/all_gather | solution.py:184
  62.1 205.1 %all-gather.38.cloned.1.call-start = ((), (), s32[]{:S(2)}) async-start(), calls=%async_computation.22 | async-start | bytes 1572864 | tf_op jit(solution)/shard_map/all_gather | solution.py:183
  62.9 263.9 %all-gather.22.cloned.1.call-start = ((), (), s32[]{:S(2)}) async-start(), calls=%async_computation.12 | async-start | bytes 2162688 | tf_op jit(solution)/shard_map/all_gather | solution.py:149
  63.6 321.3 %all-gather.28.cloned.1.call-start = ((), (), s32[]{:S(2)}) async-start(), calls=%async_computation.15 | async-start | bytes 2162688 | tf_op jit(solution)/shard_map/all_gather | solution.py:150
  64.2 414.8 %all-gather.30.cloned.1.call-start = ((), (), s32[]{:S(2)}) async-start(), calls=%async_computation.16 | async-start | bytes 8650752 | tf_op jit(solution)/shard_map/all_gather | solution.py:151
  65.0 492.4 %all-gather.32.cloned.1.call-start = ((), (), s32[]{:S(2)}) async-start(), calls=%async_computation.17 | async-start | bytes 8650752 | tf_op jit(solution)/shard_map/all_gather | solution.py:152
  65.5 615.5 %all-gather.36.cloned.1.call-start = ((), (), s32[]{:S(2)}) async-start(), calls=%async_computation.19 | async-start | bytes 4325376 | tf_op jit(solution)/shard_map/all_gather | solution.py:153
  66.9 588.2 %collective-permute-start.1 = (bf16[1,1,1024]{2,1,0:T(2,128)(2,1)}, bf16[1,1,1024]{2,1,0:T(2,128)(2,1)}, u32[]{:S(2)}, u32[]{:S(2)}) collective-permute-start(bf16[1,1,1024]{2,1,0:T(2,128)(2,1)} %slice.169), channel_id=1, source_target_pairs={{0,1},{2,3},{4,5},{6,7},{8,9},{10,11},{12,13},{14,15},{16,17},{18,... | collective-permute-start | bytes 6152 | tf_op jit(solution)/shard_map/ppermute | solution.py:23
  73.0 607.0 %collective-permute-start = (bf16[1,1,1024]{2,1,0:T(2,128)(2,1)}, bf16[1,1,1024]{2,1,0:T(2,128)(2,1)}, u32[]{:S(2)}, u32[]{:S(2)}) collective-permute-start(bf16[1,1,1024]{2,1,0:T(2,128)(2,1)} %slice.168), channel_id=1, source_target_pairs={{0,1},{2,3},{4,5},{6,7},{8,9},{10,11},{12,13},{14,15},{16,17},{18,... | collective-permute-start | bytes 6152 | tf_op jit(solution)/shard_map/ppermute | solution.py:23
  74.9 638.9 %reduce-scatter.18.cloned.1.call-start = ((), (), s32[]{:S(2)}) async-start(), calls=%async_computation.21 | async-start | bytes 1572864 | tf_op jit(solution)/shard_map/reduce_scatter | solution.py:273
  675.3 177.7 %reduce-scatter.36.cloned.1.call-start = ((), (), s32[]{:S(2)}) async-start(), calls=%async_computation.34 | async-start | bytes 540672
  710.5 266.7 %reduce-scatter.34.cloned.1.call-start = ((), (), s32[]{:S(2)}) async-start(), calls=%async_computation.33 | async-start | bytes 540672
  723.2 435.8 %reduce-scatter.32.cloned.1.call-start = ((), (), s32[]{:S(2)}) async-start(), calls=%async_computation.32 | async-start | bytes 8650752 | tf_op jit(solution)/shard_map/reduce_scatter | solution.py:305
  731.4 573.7 %reduce-scatter.26.cloned.1.call-start = ((), (), s32[]{:S(2)}) async-start(), calls=%async_computation.29 | async-start | bytes 4325376 | tf_op jit(solution)/shard_map/reduce_scatter | solution.py:302
  737.0 710.2 %reduce-scatter.24.cloned.1.call-start = ((), (), s32[]{:S(2)}) async-start(), calls=%async_computation.28 | async-start | bytes 4325376 | tf_op jit(solution)/shard_map/reduce_scatter | solution.py:301
  764.6 823.9 %reduce-scatter.20.cloned.1.call-start = ((), (), s32[]{:S(2)}) async-start(), calls=%async_computation.26 | async-start | bytes 4325376 | tf_op jit(solution)/shard_map/reduce_scatter | solution.py:299
  769.4 961.0 %reduce-scatter.22.cloned.1.call-start = ((), (), s32[]{:S(2)}) async-start(), calls=%async_computation.27 | async-start | bytes 4325376 | tf_op jit(solution)/shard_map/reduce_scatter | solution.py:300
  797.0 1290.2 %reduce-scatter.30.cloned.1.call-start = ((), (), s32[]{:S(2)}) async-start(), calls=%async_computation.31 | async-start | bytes 17301504 | tf_op jit(solution)/shard_map/reduce_scatter | solution.py:304
  819.5 1629.1 %reduce-scatter.28.cloned.1.call-start = ((), (), s32[]{:S(2)}) async-start(), calls=%async_computation.30 | async-start | bytes 17301504 | tf_op jit(solution)/shard_map/reduce_scatter | solution.py:303
  (143 other events, 3802.8 us)
Sparse Core Ops, SparseCore 0:
  11.0 59.1 all-gather.23
  72.4 20.1 all-gather.33
  94.7 21.3 all-gather.43
  117.4 21.2 all-gather.41
  141.6 56.4 all-gather.25
  200.1 20.1 all-gather.19
  222.4 21.2 all-gather.39
  245.9 21.2 all-gather.37
  270.2 56.4 all-gather.21
  329.6 55.3 all-gather.27
  387.8 91.1 all-gather.29
  481.8 75.4 all-gather.31
  560.3 60.6 all-gather.35
  655.2 19.2 reduce-scatter.17
  676.7 20.3 reduce-scatter.15
  710.6 134.2 reduce-scatter.35
  847.2 130.0 reduce-scatter.33
  979.9 179.0 reduce-scatter.31
  1161.9 143.1 reduce-scatter.25
  1307.8 139.3 reduce-scatter.23
  1450.1 138.3 reduce-scatter.19
  1591.4 139.0 reduce-scatter.21
  1733.3 353.8 reduce-scatter.29
  2089.9 358.6 reduce-scatter.27
where the time goes:
time: 2460 us
  waiting for transfers between devices  1990 us (81%)
  matrix products  296 us (12%)
  other arithmetic  58.4 us (2%)
  local copies, waits for them, and re-layouts  44.4 us (2%)
  blocking collectives  42 us (2%)
    reduce_scatter x1, waiting for transfers between devices, local(): lax.psum_scatter(micro_grads[6], ('dp', 'tm'), scatter_dimension=1, tiled...  361 us
    reduce_scatter x1, waiting for transfers between devices, local(): lax.psum_scatter(micro_grads[7], ('dp', 'tm'), scatter_dimension=1, tiled...  357 us
    reduce_scatter x1, waiting for transfers between devices, local(): lax.psum_scatter(micro_grads[8], ('dp', 'tm'), scatter_dimension=1, tiled...  181 us
    reduce_scatter x1, waiting for transfers between devices, local(): lax.psum_scatter(micro_grads[5], ('dp', 'tm'), scatter_dimension=1, tiled...  146 us
    reduce_scatter x1, waiting for transfers between devices, local(): lax.psum_scatter(micro_grads[4], ('dp', 'tm'), scatter_dimension=1, tiled...  142 us
    reduce_scatter x1, waiting for transfers between devices, local(): lax.psum_scatter(micro_grads[3], ('dp', 'tm'), scatter_dimension=1, tiled...  142 us
    reduce_scatter x1, waiting for transfers between devices, local(): lax.psum_scatter(micro_grads[2], ('dp', 'tm'), scatter_dimension=1, tiled...  141 us
    unnamed x26, waiting for transfers between devices  123 us
  transfers between devices with their start and end apart: 28, of which 19 were waited for; matrix products, arithmetic and copies ran while one was open for 15% of the time, Pallas kernels for 0%

commit v1 on v0

v1 whole, which is shorter than its diff:
```python
import math

import jax
import jax.numpy as jnp
from jax import lax
from jax.experimental import pallas as pl
from jax.experimental.pallas import tpu as pltpu
from jax.sharding import PartitionSpec as P

H = 8
DH = 128
MEM = 512
CMEM = 512
COMP = 2

EPSILON = 1e-05
ROPE_BASE = 10000.0
NEG_LARGE = -1e30
SCALE = 1.0 / math.sqrt(DH)
BOTH = ("dp", "tm")
LOW = jnp.bfloat16
F32 = jnp.float32


def bit_of(bit):
    return (lax.axis_index("dp") * lax.axis_size("tm") + lax.axis_index("tm")) >> bit & 1


def swap(value, bit):
    count = lax.axis_size(BOTH)
    return lax.ppermute(value, BOTH, [(i, i ^ (1 << bit)) for i in range(count)])


def bit_count():
    return lax.axis_size(BOTH).bit_length() - 1


def gather_order(last):
    high = list(range(bit_count() - 1, 2, -1))
    return {"y": high + [0, 2, 1], "x": high + [2, 0, 1], "x_first": [0] + high + [2, 1]}[last]


def gather(shard, order):
    held, done = shard, []
    for bit in order:
        other = swap(held, bit)
        mine = bit_of(bit) == 1
        axis = 1 + sum(1 for d in done if d > bit)
        held = jnp.stack(
            [jnp.where(mine, other, held), jnp.where(mine, held, other)], axis=axis
        )
        done.append(bit)
    return held.reshape(shard.shape[0], -1, shard.shape[2])


def scatter(whole, order, kept=LOW):
    count = lax.axis_size(BOTH)
    bits = bit_count()
    held = whole.reshape((2,) * bits + (whole.shape[0] // count, whole.shape[1]))
    left = list(range(bits))
    for bit in order:
        axis = sum(1 for d in left if d > bit)
        mine = bit_of(bit)
        other = swap(lax.dynamic_index_in_dim(held, 1 - mine, axis, keepdims=False), bit)
        keep = lax.dynamic_index_in_dim(held, mine, axis, keepdims=False)
        left.remove(bit)
        held = keep.astype(F32) + other.astype(F32)
        if left:
            held = held.astype(kept)
    return held


def scatter_order(first):
    high = list(range(3, bit_count()))
    return {"y": [1, 2, 0] + high, "x": [1, 0, 2] + high}[first]


def norm_parts(values):
    centre = values - jnp.mean(values, axis=-1, keepdims=True)
    spread = jnp.mean(centre * centre, axis=-1, keepdims=True)
    rate = lax.rsqrt(spread + EPSILON)
    return centre * rate, rate


def norm_back(grad, unit, rate, gain):
    scaled = grad * gain
    return rate * (
        scaled
        - jnp.mean(scaled, axis=-1, keepdims=True)
        - unit * jnp.mean(scaled * unit, axis=-1, keepdims=True)
    )


def turn_tables(positions):
    half = DH // 2
    frequency = jnp.exp(jnp.arange(half, dtype=F32) * (-2.0 * math.log(ROPE_BASE) / DH))
    angles = positions.astype(F32)[:, None] * frequency[None, :]
    cosine, sine = jnp.cos(angles), jnp.sin(angles)
    return (
        jnp.concatenate([cosine, cosine], axis=1),
        jnp.concatenate([-sine, sine], axis=1),
    )


def turned(values, cosine, sine):
    return values * cosine + pltpu.roll(values, DH // 2, 1) * sine


def unturned(values, cosine, sine):
    return values * cosine - pltpu.roll(values, DH // 2, 1) * sine


def dot_nt(left, right):
    return lax.dot_general(left, right, (((1,), (1,)), ((), ())), preferred_element_type=F32)


def dot_nn(left, right):
    return lax.dot_general(left, right, (((1,), (0,)), ((), ())), preferred_element_type=F32)


def dot_tn(left, right):
    return lax.dot_general(left, right, (((0,), (0,)), ((), ())), preferred_element_type=F32)


def attend_kernel(
    late, q_lin, ka_lin, kb_lin, va, vb, cos_a, sin_a, cos_b, sin_b,
    context, q_out, ka_out, kb_out, pa_out, pb_out,
):
    rows = q_lin.shape[0]
    keys = ka_lin.shape[0]
    lead = keys - rows
    query = turned(q_lin[...], cos_a[lead:, :], sin_a[lead:, :]).astype(LOW)
    key_a = turned(ka_lin[...], cos_a[...], sin_a[...]).astype(LOW)
    key_b = turned(kb_lin[...], cos_b[...], sin_b[...]).astype(LOW)
    q_out[...] = query
    ka_out[...] = key_a
    kb_out[...] = key_b
    score_a = dot_nt(key_a, query) * SCALE
    score_b = dot_nt(key_b, query) * SCALE
    key_at = lax.broadcasted_iota(jnp.int32, (keys, rows), 0) - lead
    query_at = lax.broadcasted_iota(jnp.int32, (keys, rows), 1)
    score_a = jnp.where(key_at <= query_at, score_a, NEG_LARGE)
    score_b = jnp.where(key_at < late[0] * rows, score_b, NEG_LARGE)
    top = jnp.maximum(
        jnp.max(score_a, axis=0, keepdims=True), jnp.max(score_b, axis=0, keepdims=True)
    )
    exp_a = jnp.exp(score_a - top)
    exp_b = jnp.exp(score_b - top)
    total = jnp.sum(exp_a, axis=0, keepdims=True) + jnp.sum(exp_b, axis=0, keepdims=True)
    share = 1.0 / total
    attn_a = (exp_a * share).astype(LOW)
    attn_b = (exp_b * share).astype(LOW)
    pa_out[0, 0] = attn_a
    pb_out[0, 0] = attn_b
    mixed = dot_tn(va[...], attn_a) + dot_tn(vb[...], attn_b)
    context[...] = mixed.T.astype(LOW)


def attend_back_kernel(
    grad, query, ka, kb, va, vb, pa, pb, cos_a, sin_a, cos_b, sin_b,
    gq_out, gka_out, gkb_out, gva_out, gvb_out,
):
    rows = query.shape[0]
    keys = ka.shape[0]
    lead = keys - rows
    attn_a = pa[0, 0].astype(F32)
    attn_b = pb[0, 0].astype(F32)
    back_a = dot_nt(va[...], grad[...])
    back_b = dot_nt(vb[...], grad[...])
    inner = jnp.sum(attn_a * back_a, axis=0, keepdims=True) + jnp.sum(
        attn_b * back_b, axis=0, keepdims=True
    )
    score_a = (attn_a * (back_a - inner)).astype(LOW)
    score_b = (attn_b * (back_b - inner)).astype(LOW)
    gka_out[...] = unturned(
        dot_nn(score_a, query[...]) * SCALE, cos_a[...], sin_a[...]
    ).astype(LOW)
    gkb_out[...] = unturned(
        dot_nn(score_b, query[...]) * SCALE, cos_b[...], sin_b[...]
    ).astype(LOW)
    gva_out[...] = dot_nn(pa[0, 0], grad[...]).astype(LOW)
    gvb_out[...] = dot_nn(pb[0, 0], grad[...]).astype(LOW)
    mixed = dot_tn(ka[...], score_a) + dot_tn(kb[...], score_b)
    gq_out[...] = unturned(mixed.T * SCALE, cos_a[lead:, :], sin_a[lead:, :]).astype(LOW)


def head_spec(rows):
    return pl.BlockSpec((rows, DH), lambda b, h: (b, h))


def table_spec(rows):
    return pl.BlockSpec((rows, DH), lambda b, h: (0, 0))


def attn_spec(keys, rows):
    return pl.BlockSpec((1, 1, keys, rows), lambda b, h: (b, h, 0, 0))


def attend(late, q_lin, ka_lin, kb_lin, va, vb, tables, batch):
    rows = q_lin.shape[0] // batch
    keys = ka_lin.shape[0] // batch
    width = q_lin.shape[1]
    shape = jax.ShapeDtypeStruct
    return pl.pallas_call(
        attend_kernel,
        grid=(batch, H),
        in_specs=[pl.BlockSpec(memory_space=pltpu.SMEM), head_spec(rows)]
        + [head_spec(keys)] * 4
        + [table_spec(keys)] * 4,
        out_specs=[head_spec(rows), head_spec(rows), head_spec(keys), head_spec(keys)]
        + [attn_spec(keys, rows)] * 2,
        out_shape=[shape((batch * rows, width), LOW)] * 2
        + [shape((batch * keys, width), LOW)] * 2
        + [shape((batch, H, keys, rows), LOW)] * 2,
        compiler_params=pltpu.CompilerParams(vmem_limit_bytes=40 * 2**20),
        cost_estimate=pl.CostEstimate(
            flops=8 * batch * width * rows * keys,
            bytes_accessed=40 * 2**20,
            transcendentals=2 * batch * H * rows * keys,
        ),
        name="attend",
    )(late, q_lin, ka_lin, kb_lin, va, vb, *tables)


def attend_back(grad, query, ka, kb, va, vb, pa, pb, tables, batch):
    rows = query.shape[0] // batch
    keys = ka.shape[0] // batch
    width = query.shape[1]
    shape = jax.ShapeDtypeStruct
    return pl.pallas_call(
        attend_back_kernel,
        grid=(batch, H),
        in_specs=[head_spec(rows)] * 2
        + [head_spec(keys)] * 4
        + [attn_spec(keys, rows)] * 2
        + [table_spec(keys)] * 4,
        out_specs=[head_spec(rows)] + [head_spec(keys)] * 4,
        out_shape=[shape((batch * rows, width), LOW)] + [shape((batch * keys, width), LOW)] * 4,
        compiler_params=pltpu.CompilerParams(vmem_limit_bytes=40 * 2**20),
        cost_estimate=pl.CostEstimate(
            flops=16 * batch * width * rows * keys,
            bytes_accessed=40 * 2**20,
            transcendentals=0,
        ),
        name="attend_back",
    )(grad, query, ka, kb, va, vb, pa, pb, *tables)


def local(
    hidden_in, memory, compressed_in, lengths, gain_attn, gain_ffn,
    w_query, w_key, w_value, w_out, w_up, w_down, w_compress, cot_out, cot_comp,
):
    micro, streams, block, width = hidden_in.shape
    batch = micro * streams
    rows = batch * block
    late = lax.axis_index("tm")
    windows_each = block // COMP

    hidden = hidden_in.reshape(batch, block, width)
    mem = memory.reshape(batch, -1, width)
    cmem = compressed_in.reshape(batch, -1, width)
    hidden_far = swap(hidden, 0)
    mem_far = swap(mem, 0)
    cmem_far = swap(cmem, 0)

    gains = gather(
        jnp.stack([gain_attn, gain_ffn]).reshape(2, 1, -1), gather_order("x_first")
    ).reshape(2, width).astype(F32)
    gain_first, gain_second = gains[0], gains[1]
    key_value = gather(jnp.stack([w_key.T, w_value.T]), gather_order("x_first"))
    query_out = gather(jnp.stack([w_query.T, w_out.T]), gather_order("x_first"))
    up_t = gather(w_up.T[None], gather_order("x"))[0]
    down_t = gather(w_down.T[None], gather_order("y"))[0]
    compress_t = gather(w_compress.T[None], gather_order("y"))[0]
    key_t, value_t = key_value[0], key_value[1]
    query_t, out_t = query_out[0], query_out[1]

    cmem_size, mem_size = cmem.shape[1], mem.shape[1]

    def positions(half):
        return jnp.concatenate(
            [
                COMP * (half * cmem_size + jnp.arange(cmem_size, dtype=jnp.int32) - CMEM) - MEM,
                half * mem_size + jnp.arange(mem_size, dtype=jnp.int32) - MEM,
                half * block + jnp.arange(block, dtype=jnp.int32),
            ]
        )

    tables = turn_tables(positions(late)) + turn_tables(positions(1 - late))
    lens = lengths.reshape(batch)
    query_pos = late * block + jnp.arange(block, dtype=jnp.int32)
    window_end = late * block + COMP * jnp.arange(windows_each, dtype=jnp.int32)
    row_mask = (query_pos[None, :] < lens[:, None]).astype(F32)[..., None]
    window_mask = (window_end[None, :] < lens[:, None]).astype(F32)[..., None]

    inputs = hidden.astype(F32)
    unit, rate = norm_parts(inputs)
    normed = (unit * gain_first).astype(LOW)
    unit_far, _ = norm_parts(hidden_far.astype(F32))
    normed_far = (unit_far * gain_first).astype(LOW)

    rim = normed_far[:, block - 1 :] * (late == 1).astype(LOW)
    padded = jnp.concatenate([rim, normed[:, : block - 1]], axis=1)
    windows = padded.reshape(batch * windows_each, COMP * width)
    comp_grad = (
        (cot_comp.reshape(batch, windows_each, width).astype(F32) * window_mask)
        .astype(LOW)
        .reshape(batch * windows_each, width)
    )
    compressed = dot_nt(windows, compress_t).reshape(batch, windows_each, width) * window_mask
    grad_compress = scatter(dot_tn(comp_grad, windows).astype(LOW), scatter_order("y"))
    grad_windows = dot_nn(comp_grad, compress_t).reshape(batch, block, width)
    rim_grad = swap(grad_windows[:, :1].astype(LOW), 0).astype(F32) * (late == 0).astype(F32)
    grad_shifted = jnp.concatenate([grad_windows[:, 1:], rim_grad], axis=1)

    near = jnp.concatenate([cmem, mem, normed], axis=1).reshape(-1, width)
    far = jnp.concatenate([cmem_far, mem_far, normed_far], axis=1).reshape(-1, width)
    normed = normed.reshape(rows, width)
    q_lin = dot_nt(normed, query_t)
    ka_lin = dot_nt(near, key_t)
    kb_lin = dot_nt(far, key_t)
    va = dot_nt(near, value_t).astype(LOW)
    vb = dot_nt(far, value_t).astype(LOW)
    context, query, ka, kb, pa, pb = attend(
        late.reshape(1), q_lin, ka_lin, kb_lin, va, vb, tables, batch
    )
    middle = inputs.reshape(rows, width) + dot_nt(context, out_t)

    unit_ffn, rate_ffn = norm_parts(middle)
    ffn = (unit_ffn * gain_second).astype(LOW)
    upper = dot_nt(ffn, up_t)
    slope = math.sqrt(2.0 / math.pi)
    bent = jnp.tanh(slope * (upper + 0.044715 * upper * upper * upper))
    active = (0.5 * upper * (1.0 + bent)).astype(LOW)
    gelu_slope = 0.5 * (1.0 + bent) + 0.5 * upper * (1.0 - bent * bent) * slope * (
        1.0 + 3.0 * 0.044715 * upper * upper
    )
    branch = dot_nt(active, down_t)
    live = row_mask.reshape(rows, 1)
    layer_out = ((middle + branch) * live).astype(LOW)
    grad_live = cot_out.reshape(rows, width).astype(F32) * live
    grad_branch = grad_live.astype(LOW)
    grad_upper = (dot_nn(grad_branch, down_t) * gelu_slope).astype(LOW)
    grad_down = scatter(dot_tn(grad_branch, active).astype(LOW), scatter_order("y"))
    grad_up = scatter(dot_tn(grad_upper, ffn).astype(LOW), scatter_order("x"))
    grad_ffn = dot_nn(grad_upper, up_t)
    grad_gain_ffn = jnp.sum(grad_ffn * unit_ffn, axis=0)
    grad_middle = grad_live + norm_back(grad_ffn, unit_ffn, rate_ffn, gain_second)

    grad_attended = grad_middle.astype(LOW)
    grad_out = scatter(dot_tn(grad_attended, context).astype(LOW), scatter_order("y"))
    grad_context = dot_nn(grad_attended, out_t).astype(LOW)
    gq, gka, gkb, gva, gvb = attend_back(
        grad_context, query, ka, kb, va, vb, pa, pb, tables, batch
    )
    grad_value = scatter(
        (dot_tn(gva, near) + dot_tn(gvb, far)).astype(LOW), scatter_order("x")
    )
    grad_key = scatter((dot_tn(gka, near) + dot_tn(gkb, far)).astype(LOW), scatter_order("y"))
    grad_query = scatter(dot_tn(gq, normed).astype(LOW), scatter_order("x"))

    def token_rows(values):
        return values.reshape(batch, -1, width)[:, -block:].reshape(rows, width)

    token_far = dot_nn(token_rows(gkb), key_t) + dot_nn(token_rows(gvb), value_t)
    token_back = swap(token_far.astype(LOW), 0).astype(F32)
    grad_normed = (
        dot_nn(gq, query_t)
        + dot_nn(token_rows(gka), key_t)
        + dot_nn(token_rows(gva), value_t)
        + grad_shifted.reshape(rows, width)
        + token_back
    )
    unit = unit.reshape(rows, width)
    grad_gain_attn = jnp.sum(grad_normed * unit, axis=0)
    grad_in = grad_middle + norm_back(grad_normed, unit, rate.reshape(rows, 1), gain_first)
    gain_grads = scatter(
        jnp.stack([grad_gain_attn, grad_gain_ffn], axis=1), scatter_order("x"), F32
    )

    return (
        layer_out.reshape(hidden_in.shape),
        compressed.astype(LOW).reshape(cot_comp.shape),
        grad_in.astype(LOW).reshape(hidden_in.shape),
        gain_grads[:, 0],
        gain_grads[:, 1],
        grad_query.T,
        grad_key.T,
        grad_value.T,
        grad_out.T,
        grad_up.T,
        grad_down.T,
        grad_compress.T,
    )


def solution(mesh):
    rows = P(None, "dp", "tm", None)
    columns = P(None, BOTH)
    return jax.shard_map(
        local,
        mesh=mesh,
        in_specs=(rows, rows, rows, P(None, "dp"), P(BOTH), P(BOTH))
        + (columns,) * 7
        + (rows, rows),
        out_specs=(rows, rows, rows, P(BOTH), P(BOTH)) + (columns,) * 7,
        check_vma=False,
    )
```

time: 2460 us -> 790 us (0.32)
  waiting for transfers between devices: 1990 us -> 331 us
  matrix products: 296 us -> 125 us
  starting transfers between devices: 11.3 us -> 73 us
  Pallas kernels: 0 us -> 58.5 us
  other arithmetic: 58.4 us -> 111 us
  blocking collectives: 42 us -> 0 us
  local copies, waits for them, and re-layouts: 44.4 us -> 78.9 us
    reduce_scatter x9 -> x0, waiting for transfers between devices: 1470 us -> none  [the longest x1 361 us: local(): lax.psum_scatter(micro_grads[6], ('dp', 'tm'), scatter_dimension=1, tiled...]
    all_gather x13 -> x0, waiting for transfers between devices: 394 us -> none  [the longest x1 72.2 us: local(): lax.all_gather(shards[6], ('dp', 'tm'), axis=1, tiled=True)]
    ppermute x4 -> x75, waiting for transfers between devices: 0.01 us -> 331 us  [swap(): return lax.ppermute(value, BOTH, [(i, i ^ 1 << bit) for i in range(count)])]
    dot_general x54 -> x27, matrix products: 296 us -> 125 us  [the longest x9 50.7 us: dot_nt(): lax.dot_general(left, right, (((1,), (1,)), ((), ())), preferred_element_...]
    unnamed x26 -> x0, waiting for transfers between devices: 123 us -> none
    ppermute x4 -> x75, starting transfers between devices: 9.41 us -> 73 us  [swap(): return lax.ppermute(value, BOTH, [(i, i ^ 1 << bit) for i in range(count)])]
    pallas_call x0 -> x2, Pallas kernels: none -> 58.5 us  [the longest x1 32 us: attend_back(): pl.pallas_call(attend_back_kernel, grid=(batch, H), in_specs=[head_spec(r...]
    another operation x5 -> x63, other arithmetic: 7.31 us -> 56.2 us  [the longest x61 53.1 us: gather(): jnp.stack([jnp.where(mine, other, held), jnp.where(mine, held, other)], a...]
  transfers between devices with their start and end apart: 28 -> 75, of which waited for: 19 -> 34; matrix products, arithmetic and copies ran while one was open for 15% -> 26% of each run, Pallas kernels for 0% -> 3%
where the time goes in v1:
time: 790 us; the launch traced here: 780 us
  waiting for transfers between devices  331 us (42%)
  matrix products  125 us (16%)
  other arithmetic  111 us (14%)
  local copies, waits for them, and re-layouts  78.9 us (10%)
  starting transfers between devices  73 us (9%)
  Pallas kernels  58.5 us (7%)
    ppermute x75, waiting for transfers between devices, swap(): return lax.ppermute(value, BOTH, [(i, i ^ 1 << bit) for i in range(count)])  331 us
    ppermute x75, starting transfers between devices, swap(): return lax.ppermute(value, BOTH, [(i, i ^ 1 << bit) for i in range(count)])  73 us
    another operation x61, other arithmetic, gather(): jnp.stack([jnp.where(mine, other, held), jnp.where(mine, held, other)], a...  53.1 us
    dot_general x9, matrix products, dot_nt(): lax.dot_general(left, right, (((1,), (1,)), ((), ())), preferred_element_...  50.7 us
    dot_general x9, matrix products, dot_tn(): lax.dot_general(left, right, (((0,), (0,)), ((), ())), preferred_element_...  40.9 us
    dot_general x9, matrix products, dot_nn(): lax.dot_general(left, right, (((1,), (0,)), ((), ())), preferred_element_...  33.1 us
    pallas_call x1, Pallas kernels, attend_back(): pl.pallas_call(attend_back_kernel, grid=(batch, H), in_specs=[head_spec(r...  32 us
    unnamed x228, local copies, waits for them, and re-layouts  28.2 us
  transfers between devices with their start and end apart: 75, of which 34 were waited for; matrix products, arithmetic and copies ran while one was open for 26% of the time, Pallas kernels for 3%

profile of v1, /device:TPU:0, one launch (start us, length us, event | category | flops | bytes accessed | tf_op | source)
XLA Modules:
  0.0 780.0 jit_solution(16150147380618811816)
XLA Ops:
  61.2 9.4 %collective-permute-done.29 = bf16[1,2,32,2048]{3,2,1,0:T(8,128)(2,1)S(1)} collective-permute-done((bf16[1,2,32,2048]{3,2,1,0:T(8,128)(2,1)S(1)}, bf16[1,2,32,2048]{3,2,1,0:T(8,128)(2,1)S(1)}, u32[]{:S(2)}, u32[]{:S(2)}) %collective-permute-start.29) | collective-permute-done | bytes 262176 | tf_op jit(solution)/shard_map/ppermute | solution.py:31
  74.2 9.8 %collective-permute-done.6 = bf16[2,2,32,1024]{3,2,1,0:T(8,128)(2,1)S(1)} collective-permute-done((bf16[2,2,32,1024]{3,2,1,0:T(8,128)(2,1)S(1)}, bf16[2,2,32,1024]{3,2,1,0:T(8,128)(2,1)S(1)}, u32[]{:S(2)}, u32[]{:S(2)}) %collective-permute-start.6) | collective-permute-done | bytes 262176 | tf_op jit(solution)/shard_map/ppermute | solution.py:31
  84.9 16.3 %collective-permute-done.24 = bf16[1,2,32,4096]{3,2,1,0:T(8,128)(2,1)S(1)} collective-permute-done((bf16[1,2,32,4096]{3,2,1,0:T(8,128)(2,1)S(1)}, bf16[1,2,32,4096]{3,2,1,0:T(8,128)(2,1)S(1)}, u32[]{:S(2)}, u32[]{:S(2)}) %collective-permute-start.24) | collective-permute-done | bytes 524320 | tf_op jit(solution)/shard_map/ppermute | solution.py:31
  105.8 10.2 %collective-permute-done.12 = bf16[2,2,2,32,1024]{4,3,0,2,1:T(8,128)(2,1)S(1)} collective-permute-done((bf16[2,2,2,32,1024]{4,3,0,2,1:T(8,128)(2,1)S(1)}, bf16[2,2,2,32,1024]{4,3,0,2,1:T(8,128)(2,1)S(1)}, u32[]{:S(2)}, u32[]{:S(2)}) %collective-permute-start.12) | collective-permute-done | bytes 524320 | tf_op jit(solution)/shard_map/ppermute | solution.py:31
  116.7 8.0 %collective-permute-done.7 = bf16[2,2,2,32,1024]{4,3,2,1,0:T(8,128)(2,1)S(1)} collective-permute-done((bf16[2,2,2,32,1024]{4,3,2,1,0:T(8,128)(2,1)S(1)}, bf16[2,2,2,32,1024]{4,3,2,1,0:T(8,128)(2,1)S(1)}, u32[]{:S(2)}, u32[]{:S(2)}) %collective-permute-start.7) | collective-permute-done | bytes 524320 | tf_op jit(solution)/shard_map/ppermute | solution.py:31
  156.8 16.8 %collective-permute-done.13 = bf16[2,2,2,2,32,1024]{5,4,0,3,1,2:T(8,128)(2,1)} collective-permute-done((bf16[2,2,2,2,32,1024]{5,4,0,3,1,2:T(8,128)(2,1)}, bf16[2,2,2,2,32,1024]{5,4,0,3,1,2:T(8,128)(2,1)}, u32[]{:S(2)}, u32[]{:S(2)}) %collective-permute-start.13) | collective-permute-done | bytes 1048608 | tf_op jit(solution)/shard_map/ppermute | solution.py:31
  176.8 19.1 %collective-permute-done.8 = bf16[2,2,2,2,32,1024]{5,4,3,2,1,0:T(8,128)(2,1)S(1)} collective-permute-done((bf16[2,2,2,2,32,1024]{5,4,3,2,1,0:T(8,128)(2,1)S(1)}, bf16[2,2,2,2,32,1024]{5,4,3,2,1,0:T(8,128)(2,1)S(1)}, u32[]{:S(2)}, u32[]{:S(2)}) %collective-permute-start.8) | collective-permute-done | bytes 1048608 | tf_op jit(solution)/shard_map/ppermute | solution.py:31
  197.8 20.6 %collective-permute-done.31 = bf16[1,2,2,2,32,2048]{5,4,1,2,3,0:T(8,128)(2,1)S(1)} collective-permute-done((bf16[1,2,2,2,32,2048]{5,4,1,2,3,0:T(8,128)(2,1)S(1)}, bf16[1,2,2,2,32,2048]{5,4,1,2,3,0:T(8,128)(2,1)S(1)}, u32[]{:S(2)}, u32[]{:S(2)}) %collective-permute-start.31) | collective-permute-done | bytes 1048608 | tf_op jit(solution)/shard_map/ppermute | solution.py:31
  227.7 35.7 %collective-permute-done.26 = bf16[1,2,2,2,32,4096]{5,4,3,2,1,0:T(8,128)(2,1)S(1)} collective-permute-done((bf16[1,2,2,2,32,4096]{5,4,3,2,1,0:T(8,128)(2,1)S(1)}, bf16[1,2,2,2,32,4096]{5,4,3,2,1,0:T(8,128)(2,1)S(1)}, u32[]{:S(2)}, u32[]{:S(2)}) %collective-permute-start.26) | collective-permute-done | bytes 2097184 | tf_op jit(solution)/shard_map/ppermute | solution.py:31
  281.2 7.9 %convolution_convert_fusion.3.vb = bf16[1536,1024]{1,0:T(8,128)(2,1)} fusion(bf16[1536,1024]{1,0:T(8,128)(2,1)} %bitcast.619, bf16[1024,1024]{1,0:T(8,128)(2,1)} %bitcast.610), kind=kOutput, calls=%fused_computation.40 | convolution fusion | flops 3222798336 | bytes 8388608 | tf_op jit(solution)/shard_map/dot_general | solution.py:114
  310.2 26.5 %attend.1 = (bf16[512,1024]{1,0:T(8,128)(2,1)S(1)}, bf16[512,1024]{1,0:T(8,128)(2,1)S(1)}, bf16[1536,1024]{1,0:T(8,128)(2,1)S(1)}, bf16[1536,1024]{1,0:T(8,128)(...) custom-call(s32[1]{0:T(128)} %bitcast.1.late, f32[512,1024]{1,0:T(8,128)S(1)} %fusion.106.q_lin, ...), custom_call_target="tpu_custom_call" | custom-call | flops 3221225472 | bytes 41943040 | tf_op jit(solution)/shard_map/attend/pallas_call | solution.py:204
  346.1 9.6 %collective-permute-done.72 = bf16[2,2,32,2048]{3,2,0,1:T(8,128)(2,1)S(1)} collective-permute-done((bf16[2,2,32,2048]{3,2,0,1:T(8,128)(2,1)S(1)}, bf16[2,2,32,2048]{3,2,0,1:T(8,128)(2,1)S(1)}, u32[]{:S(2)}, u32[]{:S(2)}) %collective-permute-start.72) | collective-permute-done | bytes 524320 | tf_op jit(solution)/shard_map/ppermute | solution.py:31
  376.5 7.6 pad_maximum_fusion
  389.5 7.7 pad_maximum_fusion.1
  397.2 10.4 %fusion.103 = f32[512,4096]{1,0:T(8,128)} fusion(bf16[4096,1024]{1,0:T(8,128)(2,1)} %bitcast.603, f32[512,1024]{1,0:T(8,128)S(1)} %copy-done.28, f32[1024]{0:T(1024)S(1)} %mul.399, f32[512]{0:T(512)S(1)} %add_rsqrt_fusion, f32[512]{0:T(512)S(1)} %broadcast_multiply_fusion.4), kind=kOutput, calls=%fused_computation.379 | convolution fusion | flops 4297064448 | bytes 18882560 | tf_op jit(solution)/shard_map/dot_general | solution.py:114
  407.6 11.1 %multiply_convert_fusion.2 = bf16[512,1024]{1,0:T(8,128)(2,1)} fusion(f32[512,1024]{1,0:T(8,128)S(1)} %copy-done.28, bf16[1024,4096]{1,0:T(8,128)(2,1)} %bitcast.607, f32[512]{0:T(512)S(1)} %bitcast.667, f32[512,4096]{1,0:T(8,128)} %fusion.103), kind=kOutput, calls=%fused_computation.114 | convolution fusion | flops 4315414528 | bytes 19924992 | tf_op jit(solution)/shard_map/dot_general | solution.py:114
  418.7 12.5 %fusion.6 = bf16[512,4096]{1,0:T(8,128)(2,1)S(1)} fusion(f32[512,4096]{1,0:T(8,128)} %fusion.103, bf16[512,1024]{1,0:T(8,128)(2,1)S(1)} %bitcast.640, bf16[1024,4096]{1,0:T(8,128)(2,1)} %bitcast.608), kind=kOutput, calls=%fused_computation.8 | convolution fusion | flops 4334813184 | bytes 22020096 | tf_op jit(solution)/shard_map/dot_general | solution.py:118
  462.1 32.0 %attend_back.1 = (bf16[512,1024]{1,0:T(8,128)(2,1)S(1)}, bf16[1536,1024]{1,0:T(8,128)(2,1)S(1)}, bf16[1536,1024]{1,0:T(8,128)(2,1)S(1)}, bf16[1536,1024]{1,0:T(8,128)(2,1)S(1)}, bf16[1536,1024]{1,0:T(8,128)(2,1)}) custom-call(bf16[512,1024]{1,0:T(8,128)(2,1)S(1)} %copy-done.2, bf16[512,1024]{1,0:T(8,128)(2,1)S(1)} %get-tuple-element.24.query, ...), custom_call_target="tpu_custom_call" | custom-call | flops 6442450944 | bytes 41943040 | tf_op jit(solution)/shard_map/attend_back/pallas_call | solution.py:230
  594.2 10.3 %collective-permute-done.51 = bf16[2,2,2,32,1024]{4,3,0,1,2:T(8,128)(2,1)S(1)} collective-permute-done((bf16[2,2,2,32,1024]{4,3,0,1,2:T(8,128)(2,1)S(1)}, bf16[2,2,2,32,1024]{4,3,0,1,2:T(8,128)(2,1)S(1)}, u32[]{:S(2)}, u32[]{:S(2)}) %collective-permute-start.51) | collective-permute-done | bytes 524320 | tf_op jit(solution)/shard_map/ppermute | solution.py:31
  640.6 39.4 %collective-permute-done.42 = bf16[2,2,32,1024]{3,2,0,1:T(8,128)(2,1)S(1)} collective-permute-done((bf16[2,2,32,1024]{3,2,0,1:T(8,128)(2,1)S(1)}, bf16[2,2,32,1024]{3,2,0,1:T(8,128)(2,1)S(1)}, u32[]{:S(2)}, u32[]{:S(2)}) %collective-permute-start.42) | collective-permute-done | bytes 262176 | tf_op jit(solution)/shard_map/ppermute | solution.py:31
  693.3 38.9 %collective-permute-done.61 = bf16[2,2,2,128,1024]{3,4,0,1,2:T(8,128)(2,1)S(1)} collective-permute-done((bf16[2,2,2,128,1024]{3,4,0,1,2:T(8,128)(2,1)S(1)}, bf16[2,2,2,128,1024]{3,4,0,1,2:T(8,128)(2,1)S(1)}, u32[]{:S(2)}, u32[]{:S(2)}) %collective-permute-start.61) | collective-permute-done | bytes 2097184 | tf_op jit(solution)/shard_map/ppermute | solution.py:31
  733.8 11.3 %collective-permute-done.67 = bf16[2,2,32,4096]{3,2,0,1:T(8,128)(2,1)S(1)} collective-permute-done((bf16[2,2,32,4096]{3,2,0,1:T(8,128)(2,1)S(1)}, bf16[2,2,32,4096]{3,2,0,1:T(8,128)(2,1)S(1)}, u32[]{:S(2)}, u32[]{:S(2)}) %collective-permute-start.67) | collective-permute-done | bytes 1048608 | tf_op jit(solution)/shard_map/ppermute | solution.py:31
  748.7 9.9 %collective-permute-done.68 = bf16[2,32,4096]{2,1,0:T(8,128)(2,1)S(1)} collective-permute-done((bf16[2,32,4096]{2,1,0:T(8,128)(2,1)S(1)}, bf16[2,32,4096]{2,1,0:T(8,128)(2,1)S(1)}, u32[]{:S(2)}, u32[]{:S(2)}) %collective-permute-start.68) | collective-permute-done | bytes 524320 | tf_op jit(solution)/shard_map/ppermute | solution.py:31
  770.8 8.2 %collective-permute-done.64 = bf16[128,1024]{0,1:T(8,128)(2,1)S(1)} collective-permute-done((bf16[128,1024]{0,1:T(8,128)(2,1)S(1)}, bf16[128,1024]{0,1:T(8,128)(2,1)S(1)}, u32[]{:S(2)}, u32[]{:S(2)}) %collective-permute-start.64) | collective-permute-done | bytes 262176 | tf_op jit(solution)/shard_map/ppermute | solution.py:31
  (604 shorter events, 387.8 us)
Async XLA Ops:
  46.7 99.9 %collective-permute-start.16 = (bf16[2,256,1024]{2,1,0:T(8,128)(2,1)}, bf16[2,256,1024]{2,1,0:T(8,128)(2,1)}, u32[]{:S(2)}, u32[]{:S(2)}) collective-permute-start(bf16[2,256,1024]{2,1,0:T(8,128)(2,1)} %bitcast.646), channel_id=1, source_target_pairs={{0,1},{1,0},{2,3},{3,2},{4,5},{5,4},{6,7},{7,6},{8,9},{9,8},{10,11... | collective-permute-start | bytes 3145736 | tf_op jit(solution)/shard_map/ppermute | solution.py:31
  48.1 99.3 %collective-permute-start.15 = (bf16[2,256,1024]{2,1,0:T(8,128)(2,1)}, bf16[2,256,1024]{2,1,0:T(8,128)(2,1)}, u32[]{:S(2)}, u32[]{:S(2)}) collective-permute-start(bf16[2,256,1024]{2,1,0:T(8,128)(2,1)} %bitcast.648), channel_id=1, source_target_pairs={{0,1},{1,0},{2,3},{3,2},{4,5},{5,4},{6,7},{7,6},{8,9},{9,8},{10,11... | collective-permute-start | bytes 3145736 | tf_op jit(solution)/shard_map/ppermute | solution.py:31
  50.7 79.8 %collective-permute-start.17 = (bf16[2,256,1024]{2,1,0:T(8,128)(2,1)S(1)}, bf16[2,256,1024]{2,1,0:T(8,128)(2,1)S(1)}, u32[]{:S(2)}, u32[]{:S(2)}) collective-permute-start(bf16[2,256,1024]{2,1,0:T(8,128)(2,1)S(1)} %bitcast.597), channel_id=1, source_target_pairs={{0,1},{1,0},{2,3},{3,2},{4,5},{5,4},{6,7},{7,6},{8,9},{9,8},{10,11... | collective-permute-start | bytes 3145736 | tf_op jit(solution)/shard_map/ppermute | solution.py:31
  146.5 49.4 %collective-permute-start.8 = (bf16[2,2,2,2,32,1024]{5,4,3,2,1,0:T(8,128)(2,1)S(1)}, bf16[2,2,2,2,32,1024]{5,4,3,2,1,0:T(8,128)(2,1)S(1)}, u32[]{:S(2)}, u32[]{:S(2)}) collective-permute-start(bf16[2,2,2,2,32,1024]{5,4,3,2,1,0:T(8,128)(2,1)S(1)} %copy-done.81), channel_id=1, source_target_pairs={{0,4},{1,5},{2,6},{3,7},{4,0},{5,1},{6,2},{7,3},{8,12},{9,13},{10,... | collective-permute-start | bytes 3145736 | tf_op jit(solution)/shard_map/ppermute | solution.py:31
  147.5 71.0 %collective-permute-start.31 = (bf16[1,2,2,2,32,2048]{5,4,1,2,3,0:T(8,128)(2,1)S(1)}, bf16[1,2,2,2,32,2048]{5,4,1,2,3,0:T(8,128)(2,1)S(1)}, u32[]{:S(2)}, u32[]{:S(2)}) collective-permute-start(bf16[1,2,2,2,32,2048]{5,4,1,2,3,0:T(8,128)(2,1)S(1)} %copy-done.82), channel_id=1, source_target_pairs={{0,4},{1,5},{2,6},{3,7},{4,0},{5,1},{6,2},{7,3},{8,12},{9,13},{10,... | collective-permute-start | bytes 3145736 | tf_op jit(solution)/shard_map/ppermute | solution.py:31
  151.9 66.9 %collective-permute-start.70 = (bf16[2,2,2,2,32,2048]{5,4,0,1,3,2:T(8,128)(2,1)S(1)}, bf16[2,2,2,2,32,2048]{5,4,0,1,3,2:T(8,128)(2,1)S(1)}, u32[]{:S(2)}, u32[]{:S(2)}) collective-permute-start(bf16[2,2,2,2,32,2048]{5,4,0,1,3,2:T(8,128)(2,1)S(1)} %bitcast.635), channel_id=1, source_target_pairs={{0,2},{1,3},{2,0},{3,1},{4,6},{5,7},{6,4},{7,5},{8,10},{9,11},{10,... | collective-permute-start | bytes 6291464 | tf_op jit(solution)/shard_map/ppermute | solution.py:31
  153.6 68.5 %collective-permute-start.21 = (bf16[1,2,2,2,128,1024]{5,4,3,2,1,0:T(8,128)(2,1)S(1)}, bf16[1,2,2,2,128,1024]{5,4,3,2,1,0:T(8,128)(2,1)S(1)}, u32[]{:S(2)}, u32[]{:S(2)}) collective-permute-start(bf16[1,2,2,2,128,1024]{5,4,3,2,1,0:T(8,128)(2,1)S(1)} %pad_maximum_fusion.11), channel_id=1, source_target_pairs={{0,1},{1,0},{2,3},{3,2},{4,5},{5,4},{6,7},{7,6},{8,9},{9,8},{10,11... | collective-permute-start | bytes 6291464 | tf_op jit(solution)/shard_map/ppermute | solution.py:31
  173.6 89.8 %collective-permute-start.26 = (bf16[1,2,2,2,32,4096]{5,4,3,2,1,0:T(8,128)(2,1)S(1)}, bf16[1,2,2,2,32,4096]{5,4,3,2,1,0:T(8,128)(2,1)S(1)}, u32[]{:S(2)}, u32[]{:S(2)}) collective-permute-start(bf16[1,2,2,2,32,4096]{5,4,3,2,1,0:T(8,128)(2,1)S(1)} %pad_maximum_fusion.12), channel_id=1, source_target_pairs={{0,4},{1,5},{2,6},{3,7},{4,0},{5,1},{6,2},{7,3},{8,12},{9,13},{10,... | collective-permute-start | bytes 6291464 | tf_op jit(solution)/shard_map/ppermute | solution.py:31
  196.0 70.9 %collective-permute-start.14 = (bf16[2,2,2,2,2,32,1024]{6,5,0,4,1,2,3:T(8,128)(2,1)S(1)}, bf16[2,2,2,2,2,32,1024]{6,5,0,4,1,2,3:T(8,128)(2,1)S(1)}, u32[]{:S(2)}, u32[]{:S(2)}) collective-permute-start(bf16[2,2,2,2,2,32,1024]{6,5,0,4,1,2,3:T(8,128)(2,1)S(1)} %pad_maximum_fusion.10), channel_id=1, source_target_pairs={{0,2},{1,3},{2,0},{3,1},{4,6},{5,7},{6,4},{7,5},{8,10},{9,11},{10,... | collective-permute-start | bytes 6291464 | tf_op jit(solution)/shard_map/ppermute | solution.py:31
  218.4 87.2 %collective-permute-start.9 = (bf16[2,2,2,2,2,32,1024]{6,5,4,3,2,1,0:T(8,128)(2,1)}, bf16[2,2,2,2,2,32,1024]{6,5,4,3,2,1,0:T(8,128)(2,1)}, u32[]{:S(2)}, u32[]{:S(2)}) collective-permute-start(bf16[2,2,2,2,2,32,1024]{6,5,4,3,2,1,0:T(8,128)(2,1)} %pad_maximum_fusion.9), channel_id=1, source_target_pairs={{0,2},{1,3},{2,0},{3,1},{4,6},{5,7},{6,4},{7,5},{8,10},{9,11},{10,... | collective-permute-start | bytes 6291464 | tf_op jit(solution)/shard_map/ppermute | solution.py:31
  218.8 52.3 %collective-permute-start.32 = (bf16[1,2,2,2,2,32,2048]{6,5,1,2,4,3,0:T(8,128)(2,1)S(1)}, bf16[1,2,2,2,2,32,2048]{6,5,1,2,4,3,0:T(8,128)(2,1)S(1)}, u32[]{:S(2)}, u32[]{:S(2)}) collective-permute-start(bf16[1,2,2,2,2,32,2048]{6,5,1,2,4,3,0:T(8,128)(2,1)S(1)} %pad_maximum_fusion.13), channel_id=1, source_target_pairs={{0,2},{1,3},{2,0},{3,1},{4,6},{5,7},{6,4},{7,5},{8,10},{9,11},{10,... | collective-permute-start | bytes 6291464 | tf_op jit(solution)/shard_map/ppermute | solution.py:31
  222.6 117.0 %collective-permute-start.71 = (bf16[2,2,2,32,2048]{4,3,0,1,2:T(8,128)(2,1)}, bf16[2,2,2,32,2048]{4,3,0,1,2:T(8,128)(2,1)}, u32[]{:S(2)}, u32[]{:S(2)}) collective-permute-start(bf16[2,2,2,32,2048]{4,3,0,1,2:T(8,128)(2,1)} %dynamic-slice_bitcast_fusion.2), channel_id=1, source_target_pairs={{0,4},{1,5},{2,6},{3,7},{4,0},{5,1},{6,2},{7,3},{8,12},{9,13},{10,... | collective-permute-start | bytes 3145736 | tf_op jit(solution)/shard_map/ppermute | solution.py:31
  263.4 107.8 %collective-permute-start.22 = (bf16[1,2,2,2,2,128,1024]{6,5,4,3,2,1,0:T(8,128)(2,1)}, bf16[1,2,2,2,2,128,1024]{6,5,4,3,2,1,0:T(8,128)(2,1)}, u32[]{:S(2)}, u32[]{:S(2)}) collective-permute-start(bf16[1,2,2,2,2,128,1024]{6,5,4,3,2,1,0:T(8,128)(2,1)} %pad_maximum_fusion.2), channel_id=1, source_target_pairs={{0,2},{1,3},{2,0},{3,1},{4,6},{5,7},{6,4},{7,5},{8,10},{9,11},{10,... | collective-permute-start | bytes 12582920 | tf_op jit(solution)/shard_map/ppermute | solution.py:31
  266.9 117.2 %collective-permute-start.27 = (bf16[1,2,2,2,2,32,4096]{6,5,4,3,2,1,0:T(8,128)(2,1)}, bf16[1,2,2,2,2,32,4096]{6,5,4,3,2,1,0:T(8,128)(2,1)}, u32[]{:S(2)}, u32[]{:S(2)}) collective-permute-start(bf16[1,2,2,2,2,32,4096]{6,5,4,3,2,1,0:T(8,128)(2,1)} %pad_maximum_fusion.3), channel_id=1, source_target_pairs={{0,2},{1,3},{2,0},{3,1},{4,6},{5,7},{6,4},{7,5},{8,10},{9,11},{10,... | collective-permute-start | bytes 12582920 | tf_op jit(solution)/shard_map/ppermute | solution.py:31
  280.7 77.1 %collective-permute-start.33 = (bf16[2,1,1024]{2,1,0:T(2,128)(2,1)S(1)}, bf16[2,1,1024]{2,1,0:T(2,128)(2,1)S(1)}, u32[]{:S(2)}, u32[]{:S(2)}) collective-permute-start(bf16[2,1,1024]{2,1,0:T(2,128)(2,1)S(1)} %slice.101), channel_id=1, source_target_pairs={{0,1},{1,0},{2,3},{3,2},{4,5},{5,4},{6,7},{7,6},{8,9},{9,8},{10,11... | collective-permute-start | bytes 12296 | tf_op jit(solution)/shard_map/ppermute | solution.py:31
  518.5 44.8 %collective-permute-start.34 = (bf16[512,1024]{1,0:T(8,128)(2,1)}, bf16[512,1024]{1,0:T(8,128)(2,1)}, u32[]{:S(2)}, u32[]{:S(2)}) collective-permute-start(bf16[512,1024]{1,0:T(8,128)(2,1)} %add_convert_fusion.2), channel_id=1, source_target_pairs={{0,1},{1,0},{2,3},{3,2},{4,5},{5,4},{6,7},{7,6},{8,9},{9,8},{10,11... | collective-permute-start | bytes 3145736 | tf_op jit(solution)/shard_map/ppermute | solution.py:31
  556.2 72.1 %collective-permute-start.65 = (bf16[2,2,2,2,32,4096]{5,4,0,1,3,2:T(8,128)(2,1)}, bf16[2,2,2,2,32,4096]{5,4,0,1,3,2:T(8,128)(2,1)}, u32[]{:S(2)}, u32[]{:S(2)}) collective-permute-start(bf16[2,2,2,2,32,4096]{5,4,0,1,3,2:T(8,128)(2,1)} %bitcast.586), channel_id=1, source_target_pairs={{0,2},{1,3},{2,0},{3,1},{4,6},{5,7},{6,4},{7,5},{8,10},{9,11},{10,... | collective-permute-start | bytes 12582920 | tf_op jit(solution)/shard_map/ppermute | solution.py:31
  559.5 120.6 %collective-permute-start.60 = (bf16[2,2,2,2,128,1024]{4,5,0,1,2,3:T(8,128)(2,1)}, bf16[2,2,2,2,128,1024]{4,5,0,1,2,3:T(8,128)(2,1)}, u32[]{:S(2)}, u32[]{:S(2)}) collective-permute-start(bf16[2,2,2,2,128,1024]{4,5,0,1,2,3:T(8,128)(2,1)} %bitcast.202), channel_id=1, source_target_pairs={{0,2},{1,3},{2,0},{3,1},{4,6},{5,7},{6,4},{7,5},{8,10},{9,11},{10,... | collective-permute-start | bytes 12582920 | tf_op jit(solution)/shard_map/ppermute | solution.py:31
  580.6 45.7 %collective-permute-start.40 = (bf16[2,2,2,2,32,1024]{5,4,0,1,2,3:T(8,128)(2,1)S(1)}, bf16[2,2,2,2,32,1024]{5,4,0,1,2,3:T(8,128)(2,1)S(1)}, u32[]{:S(2)}, u32[]{:S(2)}) collective-permute-start(bf16[2,2,2,2,32,1024]{5,4,0,1,2,3:T(8,128)(2,1)S(1)} %bitcast.642), channel_id=1, source_target_pairs={{0,2},{1,3},{2,0},{3,1},{4,6},{5,7},{6,4},{7,5},{8,10},{9,11},{10,... | collective-permute-start | bytes 3145736 | tf_op jit(solution)/shard_map/ppermute | solution.py:31
  634.4 49.6 %collective-permute-start.66 = (bf16[2,2,2,32,4096]{4,3,0,1,2:T(8,128)(2,1)S(1)}, bf16[2,2,2,32,4096]{4,3,0,1,2:T(8,128)(2,1)S(1)}, u32[]{:S(2)}, u32[]{:S(2)}) collective-permute-start(bf16[2,2,2,32,4096]{4,3,0,1,2:T(8,128)(2,1)S(1)} %dynamic-slice_bitcast_fusion), channel_id=1, source_target_pairs={{0,4},{1,5},{2,6},{3,7},{4,0},{5,1},{6,2},{7,3},{8,12},{9,13},{10,... | collective-permute-start | bytes 6291464 | tf_op jit(solution)/shard_map/ppermute | solution.py:31
  637.5 49.5 %collective-permute-start.49 = (bf16[32,1024]{1,0:T(8,128)(2,1)S(1)}, bf16[32,1024]{1,0:T(8,128)(2,1)S(1)}, u32[]{:S(2)}, u32[]{:S(2)}) collective-permute-start(bf16[32,1024]{1,0:T(8,128)(2,1)S(1)} %dynamic-slice_bitcast_fusion.26), channel_id=1, source_target_pairs={{0,16},{1,17},{2,18},{3,19},{4,20},{5,21},{6,22},{7,23},{8,24},{9,... | collective-permute-start | bytes 196616 | tf_op jit(solution)/shard_map/ppermute | solution.py:31
  683.6 48.6 %collective-permute-start.61 = (bf16[2,2,2,128,1024]{3,4,0,1,2:T(8,128)(2,1)S(1)}, bf16[2,2,2,128,1024]{3,4,0,1,2:T(8,128)(2,1)S(1)}, u32[]{:S(2)}, u32[]{:S(2)}) collective-permute-start(bf16[2,2,2,128,1024]{3,4,0,1,2:T(8,128)(2,1)S(1)} %dynamic-slice_bitcast_fusion.1), channel_id=1, source_target_pairs={{0,1},{1,0},{2,3},{3,2},{4,5},{5,4},{6,7},{7,6},{8,9},{9,8},{10,11... | collective-permute-start | bytes 6291464 | tf_op jit(solution)/shard_map/ppermute | solution.py:31
  684.9 60.3 %collective-permute-start.67 = (bf16[2,2,32,4096]{3,2,0,1:T(8,128)(2,1)S(1)}, bf16[2,2,32,4096]{3,2,0,1:T(8,128)(2,1)S(1)}, u32[]{:S(2)}, u32[]{:S(2)}) collective-permute-start(bf16[2,2,32,4096]{3,2,0,1:T(8,128)(2,1)S(1)} %dynamic-slice_bitcast_fusion.3), channel_id=1, source_target_pairs={{0,1},{1,0},{2,3},{3,2},{4,5},{5,4},{6,7},{7,6},{8,9},{9,8},{10,11... | collective-permute-start | bytes 3145736 | tf_op jit(solution)/shard_map/ppermute | solution.py:31
  691.7 54.0 %collective-permute-start.44 = (bf16[32,1024]{1,0:T(8,128)(2,1)S(1)}, bf16[32,1024]{1,0:T(8,128)(2,1)S(1)}, u32[]{:S(2)}, u32[]{:S(2)}) collective-permute-start(bf16[32,1024]{1,0:T(8,128)(2,1)S(1)} %dynamic-slice_bitcast_fusion.27), channel_id=1, source_target_pairs={{0,16},{1,17},{2,18},{3,19},{4,20},{5,21},{6,22},{7,23},{8,24},{9,... | collective-permute-start | bytes 196616 | tf_op jit(solution)/shard_map/ppermute | solution.py:31
  (162 other events, 1697.4 us)
